TPU v7x, 256 devices: a whole 4x4x8 slice. The times are simulated.
256 devices in a mesh: ex: 4 (over y), par: 64 (over z, x, core).
Axes of the slice: x: 4, y: 4, z: 8, core: 2. Of those that a mesh axis runs over, the one named last changes fastest.
Arguments:
- train_grads: bfloat16 [128, 524288], P('ex', 'par'), may hold values from -17 to 17
- val_grads: bfloat16 [32, 524288], P('ex', 'par'), may hold values from -17 to 17
- first_moment: float32 [524288], P('par'), may hold values from -0.6 to 0.6
- second_moment: float32 [524288], P('par'), may hold values from 0.01 to 1
- row_codes: int32 [524288], P('par'), may hold values from 1 to 1864135
- col_codes: int32 [8192], replicated, may hold values from 1 to 1073741823
- mix_offset: int32 [1], replicated, may hold values from 0 to 999999
Outputs:
- train_features: float32 [128, 8192], P('ex', 'par')
- scores: float32 [128, 32], P('ex')
All inputs are finite; a program needn't handle non-finite values.
Results may differ from a plain program's by a relative error of at most 0.0029.
Values may be sent and summed in bfloat16 or wider, within the bound.
A program may use at most 64 MiB of HBM per device.

v0:
```python
import math

import jax
import jax.numpy as jnp
from jax import lax
from jax.sharding import PartitionSpec as P

K = 8192
P_SIZE = 524288


def make_tile(row_part, col_part, offset_code):
    mixed = row_part[:, None] * col_part[None, :] + offset_code
    mixed = mixed ^ mixed >> 15
    mixed = mixed * 739982445
    bits = mixed >> 16 & 1
    return (2 * bits - 1).astype(jnp.bfloat16)


def per_device(
    train_grads, val_grads, first_moment, second_moment, row_codes, col_codes, mix_offset
):
    grads = train_grads.astype(jnp.float32)
    moment_one = 0.9 * first_moment[None, :] + 0.1 * grads
    moment_two = 0.999 * second_moment[None, :] + 0.001 * grads * grads
    adam_dir = (moment_one / (jnp.sqrt(moment_two) + 1e-08)).astype(jnp.bfloat16)
    stacked = jnp.concatenate([adam_dir, val_grads], axis=0)
    train_rows = train_grads.shape[0]
    local_params = stacked.shape[1]
    block_rows = math.gcd(local_params, 1024)
    offset_code = mix_offset[0]
    factor = 1.0 / math.sqrt(P_SIZE)

    def add_block(index, total):
        first = index * block_rows
        row_part = lax.dynamic_slice_in_dim(row_codes, first, block_rows)
        grad_part = lax.dynamic_slice_in_dim(stacked, first, block_rows, 1)
        tile = make_tile(row_part, col_codes, offset_code)
        return total + lax.dot_general(
            tile, grad_part, (((0,), (1,)), ((), ())), preferred_element_type=jnp.float32
        )

    start_total = jnp.zeros((col_codes.shape[0], stacked.shape[0]), jnp.float32)
    total = lax.fori_loop(0, local_params // block_rows, add_block, start_total)
    shares = lax.psum_scatter(total * factor, "par", scatter_dimension=0, tiled=True)
    features = shares.T
    squares = lax.psum(jnp.sum(features * features, axis=1), "par")
    inverse = lax.rsqrt(squares / K + 1e-06)
    normed = features * inverse[:, None]
    train_features = normed[:train_rows]
    val_all = lax.all_gather(normed[train_rows:], "ex", axis=0, tiled=True)
    partial_value = jnp.dot(train_features, val_all.T, precision=lax.Precision.HIGHEST)
    scores = lax.psum(partial_value, "par") / K
    return (train_features, scores)


def solution(mesh):
    in_specs = (P("ex", "par"), P("ex", "par"), P("par"), P("par"), P("par"), P(), P())
    out_specs = (P("ex", "par"), P("ex", None))
    return jax.shard_map(
        per_device, mesh=mesh, in_specs=in_specs, out_specs=out_specs, check_vma=False
    )
```

profile of v0, /device:TPU:1, one launch (start us, length us, event | category | flops | bytes accessed | tf_op | source)
XLA Modules:
  0.0 646.4 jit_solution(15877119388133758035)
XLA Ops:
  7.2 0.8 broadcast_multiply_fusion.1
  8.0 1.6 fusion.21
  9.7 108.6 %while.16 = (s32[]{:T(128)}, f32[8192,40]{0,1:T(8,128)S(1)}, s32[8192]{0:T(1024)}, s32[8192]{0:T(1024)S(1)}, s32[]{:T(128)}, /*index=5*/bf16[40,8192]{1,0:T(8,12...) while((s32[]{:T(128)}, f32[8192,40]{0,1:T(8,128)S(1)}, s32[8192]{0:T(1024)}, ...), condition=%wide.region_1.0_spmd.clone, body=%wide.region_0.0_spmd.clone.sunk | while | flops 755630080 | bytes 2748593 | solution.py:44
  9.7 0.7 dynamic_slice.27
  10.4 12.8 %fusion.33 = f32[8192,40]{0,1:T(8,128)S(1)} fusion(s32[]{:T(128)} %get-tuple-element.253, s32[8192]{0:T(1024)S(1)} %get-tuple-element.252, s32[1024]{0:T(1024)S(1)} %dynamic_slice.27, f32[8192,40]{0,1:T(8,128)S(1)} %get-tuple-element.240, pred[]{:T(512)S(6)} %compare.3, bf16[40,8192]{1,0:T(8,128)(2,1)S(1)} %get-tuple-element.254, s32[]{:T(128)S(6)} %select_n.13), kind=kOutput, calls=%fused_computation.8.clone.1 | convolution fusion | flops 755630080 | bytes 2740233 | tf_op jit(solution)/shard_map/while/body/eval_jaxpr/dot_general | solution.py:39
  23.3 0.7 dynamic_slice.27
  24.0 12.8 %fusion.33 = f32[8192,40]{0,1:T(8,128)S(1)} fusion(s32[]{:T(128)} %get-tuple-element.253, s32[8192]{0:T(1024)S(1)} %get-tuple-element.252, s32[1024]{0:T(1024)S(1)} %dynamic_slice.27, f32[8192,40]{0,1:T(8,128)S(1)} %get-tuple-element.240, pred[]{:T(512)S(6)} %compare.3, bf16[40,8192]{1,0:T(8,128)(2,1)S(1)} %get-tuple-element.254, s32[]{:T(128)S(6)} %select_n.13), kind=kOutput, calls=%fused_computation.8.clone.1 | convolution fusion | flops 755630080 | bytes 2740233 | tf_op jit(solution)/shard_map/while/body/eval_jaxpr/dot_general | solution.py:39
  36.9 0.7 dynamic_slice.27
  37.6 12.8 %fusion.33 = f32[8192,40]{0,1:T(8,128)S(1)} fusion(s32[]{:T(128)} %get-tuple-element.253, s32[8192]{0:T(1024)S(1)} %get-tuple-element.252, s32[1024]{0:T(1024)S(1)} %dynamic_slice.27, f32[8192,40]{0,1:T(8,128)S(1)} %get-tuple-element.240, pred[]{:T(512)S(6)} %compare.3, bf16[40,8192]{1,0:T(8,128)(2,1)S(1)} %get-tuple-element.254, s32[]{:T(128)S(6)} %select_n.13), kind=kOutput, calls=%fused_computation.8.clone.1 | convolution fusion | flops 755630080 | bytes 2740233 | tf_op jit(solution)/shard_map/while/body/eval_jaxpr/dot_general | solution.py:39
  51.1 12.8 %fusion.33 = f32[8192,40]{0,1:T(8,128)S(1)} fusion(s32[]{:T(128)} %get-tuple-element.253, s32[8192]{0:T(1024)S(1)} %get-tuple-element.252, s32[1024]{0:T(1024)S(1)} %dynamic_slice.27, f32[8192,40]{0,1:T(8,128)S(1)} %get-tuple-element.240, pred[]{:T(512)S(6)} %compare.3, bf16[40,8192]{1,0:T(8,128)(2,1)S(1)} %get-tuple-element.254, s32[]{:T(128)S(6)} %select_n.13), kind=kOutput, calls=%fused_computation.8.clone.1 | convolution fusion | flops 755630080 | bytes 2740233 | tf_op jit(solution)/shard_map/while/body/eval_jaxpr/dot_general | solution.py:39
  64.0 0.7 dynamic_slice.27
  64.7 12.8 %fusion.33 = f32[8192,40]{0,1:T(8,128)S(1)} fusion(s32[]{:T(128)} %get-tuple-element.253, s32[8192]{0:T(1024)S(1)} %get-tuple-element.252, s32[1024]{0:T(1024)S(1)} %dynamic_slice.27, f32[8192,40]{0,1:T(8,128)S(1)} %get-tuple-element.240, pred[]{:T(512)S(6)} %compare.3, bf16[40,8192]{1,0:T(8,128)(2,1)S(1)} %get-tuple-element.254, s32[]{:T(128)S(6)} %select_n.13), kind=kOutput, calls=%fused_computation.8.clone.1 | convolution fusion | flops 755630080 | bytes 2740233 | tf_op jit(solution)/shard_map/while/body/eval_jaxpr/dot_general | solution.py:39
  77.6 0.7 dynamic_slice.27
  78.3 12.8 %fusion.33 = f32[8192,40]{0,1:T(8,128)S(1)} fusion(s32[]{:T(128)} %get-tuple-element.253, s32[8192]{0:T(1024)S(1)} %get-tuple-element.252, s32[1024]{0:T(1024)S(1)} %dynamic_slice.27, f32[8192,40]{0,1:T(8,128)S(1)} %get-tuple-element.240, pred[]{:T(512)S(6)} %compare.3, bf16[40,8192]{1,0:T(8,128)(2,1)S(1)} %get-tuple-element.254, s32[]{:T(128)S(6)} %select_n.13), kind=kOutput, calls=%fused_computation.8.clone.1 | convolution fusion | flops 755630080 | bytes 2740233 | tf_op jit(solution)/shard_map/while/body/eval_jaxpr/dot_general | solution.py:39
  91.1 0.7 dynamic_slice.27
  91.8 12.8 %fusion.33 = f32[8192,40]{0,1:T(8,128)S(1)} fusion(s32[]{:T(128)} %get-tuple-element.253, s32[8192]{0:T(1024)S(1)} %get-tuple-element.252, s32[1024]{0:T(1024)S(1)} %dynamic_slice.27, f32[8192,40]{0,1:T(8,128)S(1)} %get-tuple-element.240, pred[]{:T(512)S(6)} %compare.3, bf16[40,8192]{1,0:T(8,128)(2,1)S(1)} %get-tuple-element.254, s32[]{:T(128)S(6)} %select_n.13), kind=kOutput, calls=%fused_computation.8.clone.1 | convolution fusion | flops 755630080 | bytes 2740233 | tf_op jit(solution)/shard_map/while/body/eval_jaxpr/dot_general | solution.py:39
  105.4 12.8 %fusion.33 = f32[8192,40]{0,1:T(8,128)S(1)} fusion(s32[]{:T(128)} %get-tuple-element.253, s32[8192]{0:T(1024)S(1)} %get-tuple-element.252, s32[1024]{0:T(1024)S(1)} %dynamic_slice.27, f32[8192,40]{0,1:T(8,128)S(1)} %get-tuple-element.240, pred[]{:T(512)S(6)} %compare.3, bf16[40,8192]{1,0:T(8,128)(2,1)S(1)} %get-tuple-element.254, s32[]{:T(128)S(6)} %select_n.13), kind=kOutput, calls=%fused_computation.8.clone.1 | convolution fusion | flops 755630080 | bytes 2740233 | tf_op jit(solution)/shard_map/while/body/eval_jaxpr/dot_general | solution.py:39
  118.3 1.2 broadcast_multiply_fusion
  119.5 134.7 %reduce-scatter.2.cloned.1.call-done = f32[128,40]{0,1:T(8,128)} async-done(((f32[8192,40]{0,1:T(8,128)}), f32[128,40]{0,1:T(8,128)}) %reduce-scatter.2.cloned.1.call-update) | async-done | bytes 20496 | tf_op jit(solution)/shard_map/reduce_scatter | solution.py:45
  254.2 0.8 multiply_reduce_fusion
  255.0 129.5 %psum.14 = f32[40]{0:T(128)S(1)} all-reduce(f32[40]{0:T(128)S(1)} %multiply_reduce_fusion), channel_id=1, replica_groups=mesh['ex'=4,'par'=64] {'par'}, use_global_device_ids=true, to_apply=%region_4.0 | all-reduce | flops 40 | bytes 320 | tf_op jit(solution)/shard_map/psum | solution.py:47
  384.5 0.8 multiply_bitcast_fusion
  385.4 9.4 %all_gather.3 = f32[32,128]{1,0:T(8,128)S(1)} all-gather(f32[8,128]{1,0:T(8,128)S(1)} %slice.9), channel_id=1, replica_groups=mesh['ex'=4,'par'=64] {'ex'}, dimensions={0}, use_global_device_ids=true | all-gather | bytes 20480 | tf_op jit(solution)/shard_map/all_gather | solution.py:51
  394.9 244.0 %psum.15 = f32[32,32]{1,0:T(8,128)S(1)} all-reduce(f32[32,32]{1,0:T(8,128)S(1)} %fusion.25), channel_id=1, replica_groups=mesh['ex'=4,'par'=64] {'par'}, use_global_device_ids=true, to_apply=%region_5.0 | all-reduce | flops 1024 | bytes 8192 | tf_op jit(solution)/shard_map/psum | solution.py:53
  (17 shorter events, 2.3 us)
Async XLA Ops:
  7.2 2.5 copy-start
  7.2 2.5 copy-start.2
  7.2 247.0 %reduce-scatter.2.cloned.1.call-start = ((), (), s32[]{:S(2)}) async-start(), calls=%async_computation.1 | async-start | bytes 1331200 | tf_op jit(solution)/shard_map/reduce_scatter | solution.py:45
  385.4 254.2 %copy-start.1 = (f32[32,128]{1,0:T(8,128)}, f32[32,128]{1,0:T(8,128)S(1)}, u32[]{:S(2)}) copy-start(f32[32,128]{1,0:T(8,128)S(1)} %slice.8) | copy-start | bytes 49156
Sparse Core Ops, SparseCore 0:
  119.6 134.5 reduce-scatter.1
where the time goes:
time: 651 us; the launch traced here: 646 us
  blocking collectives  383 us (59%)
  waiting for transfers between devices  135 us (21%)
  matrix products  103 us (16%)
  between operations  14.1 us (2%)
    psum x1, blocking collectives, per_device(): scores = lax.psum(partial_value, 'par') / K  244 us
    reduce_scatter x1, waiting for transfers between devices, per_device(): lax.psum_scatter(total * factor, 'par', scatter_dimension=0, tiled=True)  135 us
    psum x1, blocking collectives, per_device(): squares = lax.psum(jnp.sum(features * features, axis=1), 'par')  130 us
    dot_general x8, matrix products, add_block(): lax.dot_general(tile, grad_part, (((0,), (1,)), ((), ())), preferred_elem...  103 us
  transfers between devices with their start and end apart: 1, of which 1 were waited for; matrix products, arithmetic and copies ran while one was open for 0% of the time, Pallas kernels for 0%

commit v1 on v0

v1 whole, which is shorter than its diff:
```python
import functools
import math

import jax
import jax.numpy as jnp
from jax import lax
from jax.experimental import pallas as pl
from jax.experimental.pallas import tpu as pltpu
from jax.sharding import PartitionSpec as P

K = 8192
P_SIZE = 524288
MESH = pl.DeviceIdType.MESH
LANES = 128
NX = 4
NC = 2
TRAIN_ROWS = 32
VAL_ROWS = 8
SIGN_FACTOR = ((739982445 << 15) + 2**31) % 2**32 - 2**31
X_LAG = 2
Y_LAG = 3


def make_entries(row_b, cols, offset, dest, depth):
    step = 128
    for first in range(0, depth, step):
        rows = row_b[first : first + step, :]
        for half, col in enumerate(cols):
            mixed = rows * col + offset
            mixed = mixed ^ (mixed >> 15)
            mixed = mixed * SIGN_FACTOR
            dest[first : first + step, half * LANES : (half + 1) * LANES] = jnp.where(
                mixed < 0, jnp.bfloat16(1), jnp.bfloat16(-1)
            )


def kernel(
    ny, nz, gen_first,
    train_ref, val_ref, m1_ref, m2_ref, rows_ref, cols_ref, off_ref,
    feat_ref, scores_ref,
    row_b, train_in, val_out, val_in, g_ref, tiles,
    core_out, core_in, own, x_out, x_in, x_sum, y_out, y_in, y_own, z_out, z_in,
    g1_out, g1_in, g2_out, g2_in,
    in_send, in_recv, in_local, core_send, core_recv, x_send, x_recv, y_send, y_recv, z_send, z_recv,
    g1_send, g1_recv, g2_send, g2_recv,
):
    y0 = lax.axis_index("ex")
    q0 = lax.axis_index("par")
    c0 = lax.rem(q0, NC)
    x0 = lax.rem(q0 // NC, NX)
    z0 = q0 // (NC * NX)
    depth = row_b.shape[0]
    all_train = ny * TRAIN_ROWS
    all_val = ny * VAL_ROWS
    all_rows = all_train + all_val
    piece = TRAIN_ROWS + all_val

    def par_of(z, x, c):
        return (z * NX + x) * NC + c

    peers = [(y0, par_of(z0, x0, 1 - c0))]
    peers += [(y0, par_of(z0, lax.rem(x0 + d, NX), c)) for d in range(1, NX) for c in (c0, 1 - c0)]
    peers += [(lax.rem(y0 + d, ny), q0) for d in range(1, ny)]
    peers += [(y0, par_of(lax.rem(z0 + d, nz), x0, c0)) for d in range(1, nz)]
    barrier = pltpu.get_barrier_semaphore()
    for peer in peers:
        pl.semaphore_signal(barrier, inc=1, device_id=peer, device_id_type=MESH)

    half = depth // 2
    for d in range(ny):
        e = lax.rem(y0 + d, ny)
        upper = val_ref[:, pl.ds(pl.multiple_of(e * depth, LANES), half)].astype(jnp.float32)
        lower = val_ref[:, pl.ds(pl.multiple_of(e * depth + half, LANES), half)].astype(jnp.float32)
        stacked = jnp.concatenate([upper, lower], axis=0).astype(jnp.bfloat16)
        if d == 0:
            val_in[y0] = stacked
        else:
            val_out[d - 1] = stacked

    def remote(src, dst, send, recv, peer):
        return pltpu.make_async_remote_copy(
            src_ref=src, dst_ref=dst, send_sem=send, recv_sem=recv, device_id=peer, device_id_type=MESH
        )

    def train_copy(d, slot):
        e = lax.rem(y0 + d, ny)
        return remote(
            train_ref.at[:, pl.ds(pl.multiple_of(e * depth, LANES), depth)],
            train_in.at[slot], in_send.at[0, d - 1], in_recv.at[0, d - 1], (e, q0),
        )

    def val_copy(d, slot):
        e = lax.rem(y0 + d, ny)
        return remote(val_out.at[d - 1], val_in.at[slot], in_send.at[1, d - 1], in_recv.at[1, d - 1], (e, q0))

    pl.semaphore_wait(barrier, len(peers))
    for d in range(1, ny):
        train_copy(d, y0).start()
        val_copy(d, y0).start()
    local_copy = pltpu.make_async_copy(
        train_ref.at[:, pl.ds(pl.multiple_of(y0 * depth, LANES), depth)], train_in.at[y0], in_local
    )
    local_copy.start()

    groups = depth // LANES
    codes = rows_ref[pl.ds(pl.multiple_of(y0 * groups, groups), groups), :].T
    for j in range(groups):
        row_b[j * LANES : (j + 1) * LANES, :] = jnp.broadcast_to(codes[:, j : j + 1], (LANES, LANES))
    offset = off_ref[0]

    order = (2, 1, 3, 0)

    def tile_features(t, step_in_chunk):
        z = lax.rem(z0 + 1 + t, nz)
        x = lax.rem(x0 + step_in_chunk, NX)
        base = par_of(z, x, 0) * LANES
        mine = cols_ref[:, pl.ds(pl.multiple_of(base + c0 * LANES, LANES), LANES)]
        other = cols_ref[:, pl.ds(pl.multiple_of(base + (1 - c0) * LANES, LANES), LANES)]
        return mine, other

    def distance(k):
        return jnp.where(k == 0, 2, jnp.where(k == 1, 1, jnp.where(k == 2, 3, 0)))

    def generate(t):
        cols = tile_features(t // NX, distance(lax.rem(t, NX)))
        make_entries(row_b, cols, offset, tiles.at[t], depth)

    lax.fori_loop(0, gen_first, lambda t, c: (generate(t), c)[1], 0)

    local_copy.wait()
    for d in range(1, ny):
        source = lax.rem(y0 + ny - d, ny)
        train_copy(d, source).wait_recv()
        val_copy(d, source).wait_recv()

    def fill(j, carry):
        vals = [[], []]
        at = pl.ds(pl.multiple_of(j * LANES, LANES), LANES)
        for e in range(ny):
            both = val_in[e, :, at].astype(jnp.float32)
            vals[0].append(both[:VAL_ROWS])
            vals[1].append(both[VAL_ROWS:])
        for h in range(2):
            block = j + h * (groups // 2)
            here = pl.ds(pl.multiple_of(block * LANES, LANES), LANES)
            there = pl.ds(pl.multiple_of(y0 * depth + block * LANES, LANES), LANES)
            m1 = 0.9 * m1_ref[:, there]
            m2 = 0.999 * m2_ref[:, there]
            for e in range(ny):
                g = train_in[e, :, here].astype(jnp.float32)
                direction = (m1 + 0.1 * g) / (jnp.sqrt(m2 + 0.001 * g * g) + 1e-08)
                g_ref[block, e * TRAIN_ROWS : (e + 1) * TRAIN_ROWS, :] = direction.astype(jnp.bfloat16)
            g_ref[block, all_train:all_rows, :] = jnp.concatenate(vals[h], axis=0).astype(jnp.bfloat16)
        return carry

    lax.fori_loop(0, groups // 2, fill, 0)

    sibling = (y0, par_of(z0, x0, 1 - c0))

    def core_copy(pair):
        return remote(core_out.at[pair], core_in.at[pair], core_send.at[pair], core_recv.at[pair], sibling)

    def x_copy(i, d):
        peer = (y0, par_of(z0, lax.rem(x0 + d, NX), c0))
        return remote(x_out.at[i, d - 1], x_in.at[i, d - 1], x_send.at[i, d - 1], x_recv.at[i, d - 1], peer)

    def y_copy(i, d):
        peer = (lax.rem(y0 + d, ny), q0)
        return remote(y_out.at[i, d - 1], y_in.at[i, d - 1], y_send.at[i, d - 1], y_recv.at[i, d - 1], peer)

    def z_copy(i):
        peer = (y0, par_of(lax.rem(z0 + 1 + i, nz), x0, c0))
        return remote(z_out.at[i], z_in.at[i], z_send.at[i], z_recv.at[i], peer)

    def multiply(pair):
        lhs = jnp.concatenate([g_ref[b] for b in range(groups)], axis=1)
        for k in range(2):
            part = jnp.dot(lhs, tiles[pair * 2 + k], preferred_element_type=jnp.float32)
            own[pair, k] = part[:, :LANES]
            core_out[pair, k] = part[:, LANES:]
        core_copy(pair).start()

    def after_core(i, second):
        pair = i * 2 + second
        core_copy(pair).wait_recv()
        for k in range(2):
            d = order[second * 2 + k]
            total = own[pair, k] + core_in[pair, k]
            if d == 0:
                own[pair, k] = total
            else:
                x_out[i, d - 1] = total.astype(jnp.bfloat16)
                x_copy(i, d).start()

    def after_x(i):
        for d in range(1, NX):
            x_copy(i, d).wait_recv()
        total = own[i * 2 + 1, 1]
        for d in range(1, NX):
            total = total + x_in[i, d - 1].astype(jnp.float32)
        x_sum[...] = total
        vals = total[all_train:]
        for d in range(1, ny):
            e = lax.rem(y0 + d, ny)
            trains = x_sum[pl.ds(pl.multiple_of(e * TRAIN_ROWS, TRAIN_ROWS), TRAIN_ROWS), :]
            y_out[i, d - 1] = jnp.concatenate([trains, vals], axis=0).astype(jnp.bfloat16)
            y_copy(i, d).start()
        trains = x_sum[pl.ds(pl.multiple_of(y0 * TRAIN_ROWS, TRAIN_ROWS), TRAIN_ROWS), :]
        y_own[i] = jnp.concatenate([trains, vals], axis=0)

    def y_total(i):
        for d in range(1, ny):
            y_copy(i, d).wait_recv()
        total = y_own[i]
        for d in range(1, ny):
            total = total + y_in[i, d - 1].astype(jnp.float32)
        return total

    def after_y(i):
        z_out[i] = y_total(i)
        z_copy(i).start()

    def chunk(i, gen):
        for second in range(2):
            if gen:
                generate(gen_first + i * 2 + second)
            multiply(i * 2 + second)
            if second == 0:
                @pl.when(i >= 1)
                def _():
                    after_core(i - 1, 1)

                @pl.when(i >= X_LAG)
                def _():
                    after_x(i - X_LAG)
            else:
                after_core(i, 0)

                @pl.when(i >= Y_LAG)
                def _():
                    after_y(i - Y_LAG)

    with_gen = (nz * NX - gen_first) // 2
    lax.fori_loop(0, with_gen, lambda i, c: (chunk(i, True), c)[1], 0)
    lax.fori_loop(with_gen, nz, lambda i, c: (chunk(i, False), c)[1], 0)
    after_core(nz - 1, 1)
    for i in range(nz - X_LAG, nz):
        after_x(i)
    for i in range(nz - Y_LAG, nz - 1):
        after_y(i)
    total = y_total(nz - 1)
    for i in range(nz - 1):
        z_copy(i).wait_recv()
        total = total + z_in[i]

    total = total * (1.0 / math.sqrt(P_SIZE))
    trains, vals = total[:TRAIN_ROWS], total[TRAIN_ROWS:]
    fold = LANES // all_val
    wide = jnp.concatenate([vals] * fold, axis=0)
    dims = (((1,), (1,)), ((), ()))
    inner = lax.dot_general(trains, wide, dims, precision=lax.Precision.HIGHEST, preferred_element_type=jnp.float32)
    val_sq = lax.dot_general(
        jnp.ones((8, LANES), jnp.float32), wide * wide, dims,
        precision=lax.Precision.HIGHEST, preferred_element_type=jnp.float32,
    )
    train_sq = jnp.broadcast_to(jnp.sum(trains * trains, axis=1, keepdims=True), (TRAIN_ROWS, LANES))
    block = lax.broadcasted_iota(jnp.int32, (8, LANES), 1) // all_val

    def packed(a):
        out = a[:8]
        for b in range(1, TRAIN_ROWS // 8):
            out = jnp.where(block == b, a[b * 8 : (b + 1) * 8], out)
        return out

    def share(message, out_ref, in_ref, send, recv, targets):
        out_ref[...] = message
        copies = [
            remote(out_ref, in_ref.at[n], send.at[n], recv.at[n], target) for n, target in enumerate(targets)
        ]
        for copy in copies:
            copy.start()
        for n, copy in enumerate(copies):
            copy.wait_recv()
            message = message + in_ref[n]
        return message, copies

    message = jnp.concatenate([packed(inner), packed(train_sq), val_sq], axis=0)
    near = [(y0, par_of(z0, lax.rem(x0 + d, NX), c)) for d in range(NX) for c in (c0, 1 - c0)][1:]
    message, copies1 = share(message, g1_out, g1_in, g1_send, g1_recv, near)
    far = [(y0, par_of(lax.rem(z0 + d, nz), x0, c0)) for d in range(1, nz)]
    message, copies2 = share(message, g2_out, g2_in, g2_send, g2_recv, far)
    train_inv = lax.rsqrt(message[8:16] / K + 1e-06)
    val_inv = lax.rsqrt(message[16:24] / K + 1e-06)
    scores = message[:8] * train_inv * val_inv * (1.0 / K)
    for b in range(TRAIN_ROWS // 8):
        at = slice(b * 8, (b + 1) * 8)
        scores_ref[at, :] = scores[:, b * all_val : (b + 1) * all_val]
        scale = jnp.broadcast_to(train_inv[:, b * all_val : b * all_val + 1], (8, LANES))
        feat_ref[at, :] = trains[at] * scale

    for d in range(1, ny):
        train_copy(d, y0).wait_send()
        val_copy(d, y0).wait_send()

    def sent(i, carry):
        core_copy(i * 2).wait_send()
        core_copy(i * 2 + 1).wait_send()
        for d in range(1, NX):
            x_copy(i, d).wait_send()
        for d in range(1, ny):
            y_copy(i, d).wait_send()
        return carry

    lax.fori_loop(0, nz, sent, 0)
    lax.fori_loop(0, nz - 1, lambda i, c: (z_copy(i).wait_send(), c)[1], 0)
    for copy in copies1 + copies2:
        copy.wait_send()


def per_device(ny, par, train, val, m1, m2, rows, cols, off):
    nz = par // (NX * NC)
    local = train.shape[1]
    depth = local // ny
    all_rows = ny * (TRAIN_ROWS + VAL_ROWS)
    piece = TRAIN_ROWS + ny * VAL_ROWS
    tiles = nz * NX
    gen_first = 2 * ((tiles * 5 // 8) // 2)
    vmem = pl.BlockSpec(memory_space=pltpu.VMEM)
    f32, bf16 = jnp.float32, jnp.bfloat16
    dma = pltpu.SemaphoreType.DMA
    return pl.pallas_call(
        functools.partial(kernel, ny, nz, gen_first),
        out_shape=(
            jax.ShapeDtypeStruct((TRAIN_ROWS, LANES), f32),
            jax.ShapeDtypeStruct((TRAIN_ROWS, ny * VAL_ROWS), f32),
        ),
        in_specs=[pl.BlockSpec(memory_space=pl.ANY)] + [vmem] * 5 + [pl.BlockSpec(memory_space=pltpu.SMEM)],
        out_specs=(vmem, vmem),
        scratch_shapes=[
            pltpu.VMEM((depth, LANES), jnp.int32),
            pltpu.VMEM((ny, TRAIN_ROWS, depth), bf16),
            pltpu.VMEM((ny - 1, 2 * VAL_ROWS, depth // 2), bf16),
            pltpu.VMEM((ny, 2 * VAL_ROWS, depth // 2), bf16),
            pltpu.VMEM((depth // LANES, all_rows, LANES), bf16),
            pltpu.VMEM((tiles, depth, 2 * LANES), bf16),
            pltpu.VMEM((2 * nz, 2, all_rows, LANES), f32),
            pltpu.VMEM((2 * nz, 2, all_rows, LANES), f32),
            pltpu.VMEM((2 * nz, 2, all_rows, LANES), f32),
            pltpu.VMEM((nz, NX - 1, all_rows, LANES), bf16),
            pltpu.VMEM((nz, NX - 1, all_rows, LANES), bf16),
            pltpu.VMEM((all_rows, LANES), f32),
            pltpu.VMEM((nz, ny - 1, piece, LANES), bf16),
            pltpu.VMEM((nz, ny - 1, piece, LANES), bf16),
            pltpu.VMEM((nz, piece, LANES), f32),
            pltpu.VMEM((nz - 1, piece, LANES), f32),
            pltpu.VMEM((nz - 1, piece, LANES), f32),
            pltpu.VMEM((24, LANES), f32),
            pltpu.VMEM((NX * NC - 1, 24, LANES), f32),
            pltpu.VMEM((24, LANES), f32),
            pltpu.VMEM((nz - 1, 24, LANES), f32),
            dma((2, ny - 1)), dma((2, ny - 1)), dma,
            dma((2 * nz,)), dma((2 * nz,)),
            dma((nz, NX - 1)), dma((nz, NX - 1)),
            dma((nz, ny - 1)), dma((nz, ny - 1)),
            dma((nz - 1,)), dma((nz - 1,)),
            dma((NX * NC - 1,)), dma((NX * NC - 1,)),
            dma((nz - 1,)), dma((nz - 1,)),
        ],
        compiler_params=pltpu.CompilerParams(
            collective_id=0, has_side_effects=True, vmem_limit_bytes=60 << 20
        ),
        name="project",
    )(
        train, val, m1.reshape(1, local), m2.reshape(1, local),
        rows.reshape(local // LANES, LANES), cols.reshape(1, cols.shape[0]), off,
    )


def solution(mesh):
    in_specs = (P("ex", "par"), P("ex", "par"), P("par"), P("par"), P("par"), P(), P())
    out_specs = (P("ex", "par"), P("ex", None))
    body = functools.partial(per_device, mesh.shape["ex"], mesh.shape["par"])
    return jax.shard_map(body, mesh=mesh, in_specs=in_specs, out_specs=out_specs, check_vma=False)
```

time: 651 us -> 67.4 us (0.10)
  blocking collectives: 383 us -> 0 us
  waiting for transfers between devices: 135 us -> 0 us
  matrix products: 103 us -> 0 us
  Pallas kernels: 0 us -> 64 us
  between operations: 14.1 us -> 1.3 us
    psum x2 -> x0, blocking collectives: 374 us -> none  [the longest x1 244 us: per_device(): scores = lax.psum(partial_value, 'par') / K]
    reduce_scatter x1 -> x0, waiting for transfers between devices: 135 us -> none  [per_device(): lax.psum_scatter(total * factor, 'par', scatter_dimension=0, tiled=True)]
    dot_general x9 -> x0, matrix products: 103 us -> none  [the longest x8 103 us: add_block(): lax.dot_general(tile, grad_part, (((0,), (1,)), ((), ())), preferred_elem...]
    pallas_call x0 -> x1, Pallas kernels: none -> 64 us  [per_device(): pl.pallas_call(functools.partial(kernel, ny, nz, gen_first), out_shape=(j...]
    all_gather x1 -> x0, blocking collectives: 9.42 us -> none  [per_device(): val_all = lax.all_gather(normed[train_rows:], 'ex', axis=0, tiled=True)]
  transfers between devices with their start and end apart: 1 -> 0, of which waited for: 1 -> 0; matrix products, arithmetic and copies ran while one was open for 0% -> 0% of each run, Pallas kernels for 0% -> 0%
where the time goes in v1:
time: 67.4 us; the launch traced here: 67.3 us
  Pallas kernels  64 us (95%)
  local copies, waits for them, and re-layouts  1.94 us (3%)
  between operations  1.3 us (2%)
    pallas_call x1, Pallas kernels, per_device(): pl.pallas_call(functools.partial(kernel, ny, nz, gen_first), out_shape=(j...  64 us
    unnamed x4, local copies, waits for them, and re-layouts  1.94 us

profile of v1, /device:TPU:1, one launch (start us, length us, event | category | flops | bytes accessed | tf_op | source)
XLA Modules:
  0.0 67.3 jit_solution(10664836496221026075)
XLA Ops:
  1.3 64.0 %project.1 = (f32[32,128]{1,0:T(8,128)}, f32[32,32]{1,0:T(8,128)}) custom-call(bf16[32,8192]{1,0:T(8,128)(2,1)} %train_ref.1, bf16[8,8192]{1,0:T(8,128)(2,1)} %val_ref.1, f32[1,8192]{1,0:T(1,128)} %bitcast.4, f32[1,8192]{1,0:T(1,128)} %bitcast.5, s32[64,128]{1,0:T(8,128)} %bitcast.6, s32[1,8192]{1,0:T(1,128)} %bitcast.7, s32[1]{0:T(128)S(6)} %copy.11.off_ref), custom_call_target="tpu_custom_call" | custom-call | tf_op jit(solution)/shard_map/project/pallas_call | solution.py:331
  65.3 0.0 copy-start
  65.3 1.3 %copy.12 = f32[32,128]{1,0:T(8,128)} copy(f32[32,128]{1,0:T(8,128)} %get-tuple-element.4) | data formatting | bytes 32768
  66.7 0.0 copy-done
  66.7 0.6 copy.13
Async XLA Ops:
  65.3 1.3 %copy-start = (f32[32,32]{1,0:T(8,128)S(1)}, f32[32,32]{1,0:T(8,128)}, u32[]{:S(2)}) copy-start(f32[32,32]{1,0:T(8,128)} %get-tuple-element.5) | copy-start | bytes 12292

commit v2 on v1

v2 whole, which is shorter than its diff:
```python
import functools
import math

import jax
import jax.numpy as jnp
from jax import lax
from jax.experimental import pallas as pl
from jax.experimental.pallas import tpu as pltpu
from jax.sharding import PartitionSpec as P

K = 8192
P_SIZE = 524288
MESH = pl.DeviceIdType.MESH
LANES = 128
NX = 4
NC = 2
TRAIN_ROWS = 32
VAL_ROWS = 8
SIGN_FACTOR = ((739982445 << 15) + 2**31) % 2**32 - 2**31
CORE_LAG, RELAY_LAG, X_LAG, Y_LAG = 1, 3, 6, 9


def make_entries(row_b, cols, offset, dest, depth, start):
    step = 128
    for first in range(0, depth, step):
        rows = row_b[first : first + step, :]
        for half, col in enumerate(cols):
            mixed = rows * col + offset
            mixed = mixed ^ (mixed >> 15)
            mixed = mixed * SIGN_FACTOR
            dest[first : first + step, pl.ds(pl.multiple_of(start + half * LANES, LANES), LANES)] = jnp.where(
                mixed < 0, jnp.bfloat16(1), jnp.bfloat16(-1)
            )


def kernel(
    ny, nz, gen_early, gen_first,
    train_ref, val_ref, m1_ref, m2_ref, rows_ref, cols_ref, off_ref,
    feat_ref, scores_ref,
    row_b, train_in, val_out, val_in, g_ref, tiles,
    core_out, core_in, own, r_out, r_in, x_out, x_in, x_sum, y_out, y_in, y_own, z_out, z_in, yz_out, yz_in,
    g1_out, g1_in, g2_out, g2_in,
    in_send, in_recv, in_local, core_send, core_recv, r_send, r_recv, x_send, x_recv, y_send, y_recv, z_send, z_recv, yz_send, yz_recv,
    g1_send, g1_recv, g2_send, g2_recv,
):
    y0 = lax.axis_index("ex")
    q0 = lax.axis_index("par")
    c0 = lax.rem(q0, NC)
    x0 = lax.rem(q0 // NC, NX)
    z0 = q0 // (NC * NX)
    depth = row_b.shape[0]
    all_train = ny * TRAIN_ROWS
    all_val = ny * VAL_ROWS
    all_rows = all_train + all_val
    piece = TRAIN_ROWS + all_val

    def par_of(z, x, c):
        return (z * NX + x) * NC + c

    peers = [(y0, par_of(z0, x0, 1 - c0))]
    peers += [(y0, par_of(z0, lax.rem(x0 + d, NX), c)) for d in range(1, NX) for c in (c0, 1 - c0)]
    peers += [(lax.rem(y0 + d, ny), q0) for d in range(1, ny)]
    peers += [(y0, par_of(lax.rem(z0 + d, nz), x0, c0)) for d in range(1, nz)]
    peers += [(lax.rem(y0 + d, ny), par_of(lax.rem(z0 + 1, nz), x0, c0)) for d in range(1, ny)]
    barrier = pltpu.get_barrier_semaphore()
    for peer in peers:
        pl.semaphore_signal(barrier, inc=1, device_id=peer, device_id_type=MESH)

    def remote(src, dst, send, recv, peer):
        return pltpu.make_async_remote_copy(
            src_ref=src, dst_ref=dst, send_sem=send, recv_sem=recv, device_id=peer, device_id_type=MESH
        )

    def train_copy(d, slot):
        e = lax.rem(y0 + d, ny)
        return remote(
            train_ref.at[:, pl.ds(pl.multiple_of(e * depth, LANES), depth)],
            train_in.at[slot], in_send.at[0, d - 1], in_recv.at[0, d - 1], (e, q0),
        )

    def val_copy(d, slot):
        e = lax.rem(y0 + d, ny)
        return remote(val_out.at[d - 1], val_in.at[slot], in_send.at[1, d - 1], in_recv.at[1, d - 1], (e, q0))

    groups = depth // LANES
    codes = rows_ref[pl.ds(pl.multiple_of(y0 * groups, groups), groups), :].T
    for j in range(groups):
        row_b[j * LANES : (j + 1) * LANES, :] = jnp.broadcast_to(codes[:, j : j + 1], (LANES, LANES))
    offset = off_ref[0]

    order = (2, 1, 3, 0)

    def z_distance(i):
        return nz // 2 + jnp.where(lax.rem(i, 2) == 0, i // 2, -((i + 1) // 2))

    def tile_features(t, step_in_chunk):
        z = lax.rem(z0 + z_distance(t), nz)
        x = lax.rem(x0 + step_in_chunk, NX)
        base = par_of(z, x, 0) * LANES
        mine = cols_ref[:, pl.ds(pl.multiple_of(base + c0 * LANES, LANES), LANES)]
        other = cols_ref[:, pl.ds(pl.multiple_of(base + (1 - c0) * LANES, LANES), LANES)]
        return mine, other

    def distance(k):
        return jnp.where(k == 0, 2, jnp.where(k == 1, 1, jnp.where(k == 2, 3, 0)))

    def generate(t):
        cols = tile_features(t // NX, distance(lax.rem(t, NX)))
        make_entries(row_b, cols, offset, tiles.at[t // 2], depth, lax.rem(t, 2) * (2 * LANES))

    half = depth // 2
    for d in range(ny):
        e = lax.rem(y0 + d, ny)
        upper = val_ref[:, pl.ds(pl.multiple_of(e * depth, LANES), half)].astype(jnp.float32)
        lower = val_ref[:, pl.ds(pl.multiple_of(e * depth + half, LANES), half)].astype(jnp.float32)
        stacked = jnp.concatenate([upper, lower], axis=0).astype(jnp.bfloat16)
        if d == 0:
            val_in[y0] = stacked
        else:
            val_out[d - 1] = stacked

    lax.fori_loop(0, gen_early, lambda t, c: (generate(t), c)[1], 0)
    pl.semaphore_wait(barrier, len(peers))
    for d in range(1, ny):
        train_copy(d, y0).start()
        val_copy(d, y0).start()
    local_copy = pltpu.make_async_copy(
        train_ref.at[:, pl.ds(pl.multiple_of(y0 * depth, LANES), depth)], train_in.at[y0], in_local
    )
    local_copy.start()

    lax.fori_loop(gen_early, gen_first, lambda t, c: (generate(t), c)[1], 0)

    local_copy.wait()
    for d in range(1, ny):
        source = lax.rem(y0 + ny - d, ny)
        train_copy(d, source).wait_recv()
        val_copy(d, source).wait_recv()

    def fill(j, carry):
        vals = [[], []]
        at = pl.ds(pl.multiple_of(j * LANES, LANES), LANES)
        for e in range(ny):
            both = val_in[e, :, at].astype(jnp.float32)
            vals[0].append(both[:VAL_ROWS])
            vals[1].append(both[VAL_ROWS:])
        for h in range(2):
            block = j + h * (groups // 2)
            here = pl.ds(pl.multiple_of(block * LANES, LANES), LANES)
            there = pl.ds(pl.multiple_of(y0 * depth + block * LANES, LANES), LANES)
            m1 = 0.9 * m1_ref[:, there]
            m2 = 0.999 * m2_ref[:, there]
            for e in range(ny):
                g = train_in[e, :, here].astype(jnp.float32)
                direction = (m1 + 0.1 * g) / (jnp.sqrt(m2 + 0.001 * g * g) + 1e-08)
                g_ref[block, e * TRAIN_ROWS : (e + 1) * TRAIN_ROWS, :] = direction.astype(jnp.bfloat16)
            g_ref[block, all_train:all_rows, :] = jnp.concatenate(vals[h], axis=0).astype(jnp.bfloat16)
        return carry

    lax.fori_loop(0, groups // 2, fill, 0)

    sibling = (y0, par_of(z0, x0, 1 - c0))

    def core_copy(i):
        return remote(core_out.at[i], core_in.at[i], core_send.at[i], core_recv.at[i], sibling)

    x_steps = (1, NX - 1)

    def x_peer(side):
        return (y0, par_of(z0, lax.rem(x0 + x_steps[side], NX), c0))

    def relay_copy(i, side):
        return remote(r_out.at[i, side], r_in.at[i, side], r_send.at[i, side], r_recv.at[i, side], x_peer(side))

    def x_copy(i, side):
        return remote(x_out.at[i, side], x_in.at[i, side], x_send.at[i, side], x_recv.at[i, side], x_peer(side))

    def y_copy(i, d):
        peer = (lax.rem(y0 + d, ny), q0)
        return remote(y_out.at[i, d - 1], y_in.at[i, d - 1], y_send.at[i, d - 1], y_recv.at[i, d - 1], peer)

    def z_copy(i):
        peer = (y0, par_of(lax.rem(z0 + z_distance(i), nz), x0, c0))
        return remote(z_out.at[i], z_in.at[i], z_send.at[i], z_recv.at[i], peer)

    def yz_copy(dy):
        peer = (lax.rem(y0 + dy, ny), par_of(lax.rem(z0 + nz - 1, nz), x0, c0))
        return remote(yz_out.at[dy], yz_in.at[dy], yz_send.at[dy], yz_recv.at[dy], peer)

    def multiply(i):
        lhs = jnp.concatenate([g_ref[b] for b in range(groups)], axis=1)
        for pair in range(2):
            part = jnp.dot(lhs, tiles[i * 2 + pair], preferred_element_type=jnp.float32)
            for k in range(2):
                at = 2 * k * LANES
                own[i, pair * 2 + k] = part[:, at : at + LANES]
                core_out[i, pair * 2 + k] = part[:, at + LANES : at + 2 * LANES]
        core_copy(i).start()

    upper_rows = all_rows // 2

    def piece_of(rows, dy):
        e = lax.rem(y0 + dy, ny)
        trains = rows[pl.ds(pl.multiple_of(e * TRAIN_ROWS, TRAIN_ROWS), TRAIN_ROWS), :]
        return jnp.concatenate([trains, rows[all_train:, :]], axis=0)

    def after_core(i):
        core_copy(i).wait_recv()
        for k in range(NX):
            total = own[i, k] + core_in[i, k]
            if order[k] == 2:
                r_out[i, 0] = total[:upper_rows].astype(jnp.bfloat16)
                r_out[i, 1] = total[upper_rows:].astype(jnp.bfloat16)
                relay_copy(i, 0).start()
                relay_copy(i, 1).start()
            else:
                own[i, k] = total

    def after_relay(i):
        for side in range(2):
            relay_copy(i, side).wait_recv()
            total = own[i, order.index(x_steps[side])]
            parts = [total[:upper_rows], total[upper_rows:]]
            parts[side] = parts[side] + r_in[i, side].astype(jnp.float32)
            x_out[i, side] = jnp.concatenate(parts, axis=0).astype(jnp.bfloat16)
            x_copy(i, side).start()

    def after_x(i):
        total = own[i, order.index(0)]
        for side in range(2):
            x_copy(i, side).wait_recv()
            total = total + x_in[i, side].astype(jnp.float32)
        x_sum[...] = total

        @pl.when(i != nz - 2)
        def _():
            for d in range(1, ny):
                y_out[i, d - 1] = piece_of(x_sum, d).astype(jnp.bfloat16)
                y_copy(i, d).start()
            y_own[i] = piece_of(x_sum, 0)

        @pl.when(i == nz - 2)
        def _():
            for dy in (2, 1, 3, 0):
                yz_out[dy] = piece_of(x_sum, dy).astype(jnp.bfloat16)
                yz_copy(dy).start()

    def y_total(i):
        total = y_own[i]
        for d in range(1, ny):
            y_copy(i, d).wait_recv()
            total = total + y_in[i, d - 1].astype(jnp.float32)
        return total

    def after_y(i):
        z_out[i] = y_total(i)
        z_copy(i).start()

    def stage(i, lag, work, count):
        @pl.when((i >= lag) & (i < lag + count))
        def _():
            work(i - lag)

    def passed_on(i):
        stage(i, CORE_LAG, after_core, nz)
        stage(i, Y_LAG, after_y, nz - 2)
        stage(i, X_LAG, after_x, nz)
        stage(i, RELAY_LAG, after_relay, nz)

    def with_gen(i, carry):
        for k in range(2):
            generate(gen_first + i * 2 + k)
        multiply(i)
        passed_on(i)
        return carry

    def without_gen(i, carry):
        multiply(i)
        passed_on(i)
        return carry

    def rest(i, carry):
        passed_on(i)
        return carry

    gen_steps = (nz * NX - gen_first) // 2
    lax.fori_loop(0, gen_steps, with_gen, 0)
    lax.fori_loop(gen_steps, nz, without_gen, 0)
    lax.fori_loop(nz, nz - 2 + Y_LAG, rest, 0)
    total = y_total(nz - 1)
    for i in range(nz - 2):
        z_copy(i).wait_recv()
        total = total + z_in[i]
    for dy in range(ny):
        yz_copy(dy).wait_recv()
        total = total + yz_in[dy].astype(jnp.float32)

    total = total * (1.0 / math.sqrt(P_SIZE))
    trains, vals = total[:TRAIN_ROWS], total[TRAIN_ROWS:]
    fold = LANES // all_val
    wide = jnp.concatenate([vals] * fold, axis=0)
    dims = (((1,), (1,)), ((), ()))
    inner = lax.dot_general(trains, wide, dims, precision=lax.Precision.HIGHEST, preferred_element_type=jnp.float32)
    val_sq = lax.dot_general(
        jnp.ones((8, LANES), jnp.float32), wide * wide, dims,
        precision=lax.Precision.HIGHEST, preferred_element_type=jnp.float32,
    )
    train_sq = jnp.broadcast_to(jnp.sum(trains * trains, axis=1, keepdims=True), (TRAIN_ROWS, LANES))
    block = lax.broadcasted_iota(jnp.int32, (8, LANES), 1) // all_val

    def packed(a):
        out = a[:8]
        for b in range(1, TRAIN_ROWS // 8):
            out = jnp.where(block == b, a[b * 8 : (b + 1) * 8], out)
        return out

    def share(message, out_ref, in_ref, send, recv, targets, meanwhile):
        out_ref[...] = message
        copies = [
            remote(out_ref, in_ref.at[n], send.at[n], recv.at[n], target) for n, target in enumerate(targets)
        ]
        for copy in copies:
            copy.start()
        meanwhile()
        for n, copy in enumerate(copies):
            copy.wait_recv()
            message = message + in_ref[n]
        return message, copies

    def all_sent():
        for d in range(1, ny):
            train_copy(d, y0).wait_send()
            val_copy(d, y0).wait_send()

        def sent(i, carry):
            core_copy(i).wait_send()
            for side in range(2):
                relay_copy(i, side).wait_send()
                x_copy(i, side).wait_send()
            return carry

        def yz_sent(i, carry):
            for d in range(1, ny):
                y_copy(i, d).wait_send()
            z_copy(i).wait_send()
            return carry

        lax.fori_loop(0, nz, sent, 0)
        lax.fori_loop(0, nz - 2, yz_sent, 0)
        for d in range(1, ny):
            y_copy(nz - 1, d).wait_send()
        for dy in range(ny):
            yz_copy(dy).wait_send()

    def turned(a, by):
        return jnp.concatenate([a[:, LANES - by :], a[:, : LANES - by]], axis=1)

    part = all_val // 2
    lower = lax.rem(lax.broadcasted_iota(jnp.int32, (8, LANES), 1), all_val) < part
    odd = lax.rem(block, 2) == 1
    squares = jnp.where(lower, packed(train_sq), jnp.where(odd, val_sq, turned(val_sq, part)))
    message = jnp.concatenate([packed(inner), squares], axis=0)
    near = [(y0, par_of(z0, lax.rem(x0 + d, NX), c)) for d in range(NX) for c in (c0, 1 - c0)][1:]
    message, copies1 = share(message, g1_out, g1_in, g1_send, g1_recv, near, all_sent)
    far = [(y0, par_of(lax.rem(z0 + d, nz), x0, c0)) for d in range(1, nz)]
    message, copies2 = share(message, g2_out, g2_in, g2_send, g2_recv, far, lambda: None)
    inverse = lax.rsqrt(message[8:] / K + 1e-06)
    before = turned(inverse, part)
    train_inv = jnp.where(lower, inverse, before)
    val_inv = jnp.where(
        odd, jnp.where(lower, before, inverse),
        jnp.where(lower, turned(inverse, LANES - part), turned(inverse, LANES - 2 * part)),
    )
    scores = message[:8] * train_inv * val_inv * (1.0 / K)
    for b in range(TRAIN_ROWS // 8):
        at = slice(b * 8, (b + 1) * 8)
        scores_ref[at, :] = scores[:, b * all_val : (b + 1) * all_val]
        scale = jnp.broadcast_to(train_inv[:, b * all_val : b * all_val + 1], (8, LANES))
        feat_ref[at, :] = trains[at] * scale

    for copy in copies1 + copies2:
        copy.wait_send()


def per_device(ny, par, train, val, m1, m2, rows, cols, off):
    nz = par // (NX * NC)
    local = train.shape[1]
    depth = local // ny
    all_rows = ny * (TRAIN_ROWS + VAL_ROWS)
    piece = TRAIN_ROWS + ny * VAL_ROWS
    tiles = nz * NX
    gen_early, gen_first = tiles // 4, 2 * (tiles * 13 // 32)
    vmem = pl.BlockSpec(memory_space=pltpu.VMEM)
    f32, bf16 = jnp.float32, jnp.bfloat16
    dma = pltpu.SemaphoreType.DMA
    return pl.pallas_call(
        functools.partial(kernel, ny, nz, gen_early, gen_first),
        out_shape=(
            jax.ShapeDtypeStruct((TRAIN_ROWS, LANES), f32),
            jax.ShapeDtypeStruct((TRAIN_ROWS, ny * VAL_ROWS), f32),
        ),
        in_specs=[pl.BlockSpec(memory_space=pl.ANY)] + [vmem] * 5 + [pl.BlockSpec(memory_space=pltpu.SMEM)],
        out_specs=(vmem, vmem),
        scratch_shapes=[
            pltpu.VMEM((depth, LANES), jnp.int32),
            pltpu.VMEM((ny, TRAIN_ROWS, depth), bf16),
            pltpu.VMEM((ny - 1, 2 * VAL_ROWS, depth // 2), bf16),
            pltpu.VMEM((ny, 2 * VAL_ROWS, depth // 2), bf16),
            pltpu.VMEM((depth // LANES, all_rows, LANES), bf16),
            pltpu.VMEM((tiles // 2, depth, 4 * LANES), bf16),
            pltpu.VMEM((nz, NX, all_rows, LANES), f32),
            pltpu.VMEM((nz, NX, all_rows, LANES), f32),
            pltpu.VMEM((nz, NX, all_rows, LANES), f32),
            pltpu.VMEM((nz, 2, all_rows // 2, LANES), bf16),
            pltpu.VMEM((nz, 2, all_rows // 2, LANES), bf16),
            pltpu.VMEM((nz, 2, all_rows, LANES), bf16),
            pltpu.VMEM((nz, 2, all_rows, LANES), bf16),
            pltpu.VMEM((all_rows, LANES), f32),
            pltpu.VMEM((nz, ny - 1, piece, LANES), bf16),
            pltpu.VMEM((nz, ny - 1, piece, LANES), bf16),
            pltpu.VMEM((nz, piece, LANES), f32),
            pltpu.VMEM((nz - 2, piece, LANES), f32),
            pltpu.VMEM((nz - 2, piece, LANES), f32),
            pltpu.VMEM((ny, piece, LANES), bf16),
            pltpu.VMEM((ny, piece, LANES), bf16),
            pltpu.VMEM((16, LANES), f32),
            pltpu.VMEM((NX * NC - 1, 16, LANES), f32),
            pltpu.VMEM((16, LANES), f32),
            pltpu.VMEM((nz - 1, 16, LANES), f32),
            dma((2, ny - 1)), dma((2, ny - 1)), dma,
            dma((nz,)), dma((nz,)),
            dma((nz, 2)), dma((nz, 2)),
            dma((nz, 2)), dma((nz, 2)),
            dma((nz, ny - 1)), dma((nz, ny - 1)),
            dma((nz - 2,)), dma((nz - 2,)),
            dma((ny,)), dma((ny,)),
            dma((NX * NC - 1,)), dma((NX * NC - 1,)),
            dma((nz - 1,)), dma((nz - 1,)),
        ],
        compiler_params=pltpu.CompilerParams(
            collective_id=0, has_side_effects=True, vmem_limit_bytes=60 << 20
        ),
        name="project",
    )(
        train, val, m1.reshape(1, local), m2.reshape(1, local),
        rows.reshape(local // LANES, LANES), cols.reshape(1, cols.shape[0]), off,
    )


def solution(mesh):
    in_specs = (P("ex", "par"), P("ex", "par"), P("par"), P("par"), P("par"), P(), P())
    out_specs = (P("ex", "par"), P("ex", None))
    body = functools.partial(per_device, mesh.shape["ex"], mesh.shape["par"])
    return jax.shard_map(body, mesh=mesh, in_specs=in_specs, out_specs=out_specs, check_vma=False)
```

time: 67.4 us -> 63 us (0.935)
  Pallas kernels: 64 us -> 59.6 us
    pallas_call x1, Pallas kernels: 64 us -> 59.6 us  [per_device(): pl.pallas_call(functools.partial(kernel, ny, nz, gen_early, gen_first), o...]
where the time goes in v2:
time: 63 us; the launch traced here: 62.9 us
  Pallas kernels  59.6 us (95%)
  local copies, waits for them, and re-layouts  1.94 us (3%)
  between operations  1.3 us (2%)
    pallas_call x1, Pallas kernels, per_device(): pl.pallas_call(functools.partial(kernel, ny, nz, gen_early, gen_first), o...  59.6 us
    unnamed x4, local copies, waits for them, and re-layouts  1.94 us

profile of v2, /device:TPU:1, one launch (start us, length us, event | category | flops | bytes accessed | tf_op | source)
XLA Modules:
  0.0 62.9 jit_solution(15268545896507565295)
XLA Ops:
  1.3 59.6 %project.1 = (f32[32,128]{1,0:T(8,128)}, f32[32,32]{1,0:T(8,128)}) custom-call(bf16[32,8192]{1,0:T(8,128)(2,1)} %train_ref.1, bf16[8,8192]{1,0:T(8,128)(2,1)} %val_ref.1, f32[1,8192]{1,0:T(1,128)} %bitcast.4, f32[1,8192]{1,0:T(1,128)} %bitcast.5, s32[64,128]{1,0:T(8,128)} %bitcast.6, s32[1,8192]{1,0:T(1,128)} %bitcast.7, s32[1]{0:T(128)S(6)} %copy.11.off_ref), custom_call_target="tpu_custom_call" | custom-call | tf_op jit(solution)/shard_map/project/pallas_call | solution.py:396
  60.9 0.0 copy-start
  60.9 1.3 %copy.12 = f32[32,128]{1,0:T(8,128)} copy(f32[32,128]{1,0:T(8,128)} %get-tuple-element.4) | data formatting | bytes 32768
  62.3 0.0 copy-done
  62.3 0.6 copy.13
Async XLA Ops:
  60.9 1.3 %copy-start = (f32[32,32]{1,0:T(8,128)S(1)}, f32[32,32]{1,0:T(8,128)}, u32[]{:S(2)}) copy-start(f32[32,32]{1,0:T(8,128)} %get-tuple-element.5) | copy-start | bytes 12292

commit v3 on v2

--- a/solution.py
+++ b/solution.py
@@ -33,11 +33,38 @@
             )
 
 
+def turned(a, by):
+    return jnp.concatenate([a[:, LANES - by :], a[:, : LANES - by]], axis=1)
+
+
+def lane_masks(width):
+    lane = lax.broadcasted_iota(jnp.int32, (8, LANES), 1)
+    return lax.rem(lane, width) < width // 2, lax.rem(lane // width, 2) == 1
+
+
+def finish(all_val, raw_ref, message_ref, feat_ref, scores_ref):
+    part = all_val // 2
+    lower, odd = lane_masks(all_val)
+    inverse = lax.rsqrt(message_ref[8:] / K + 1e-06)
+    before = turned(inverse, part)
+    train_inv = jnp.where(lower, inverse, before)
+    val_inv = jnp.where(
+        odd, jnp.where(lower, before, inverse),
+        jnp.where(lower, turned(inverse, LANES - part), turned(inverse, LANES - 2 * part)),
+    )
+    scores = message_ref[:8] * train_inv * val_inv * (1.0 / K)
+    for b in range(TRAIN_ROWS // 8):
+        at = slice(b * 8, (b + 1) * 8)
+        scores_ref[at, :] = scores[:, b * all_val : (b + 1) * all_val]
+        scale = jnp.broadcast_to(train_inv[:, b * all_val : b * all_val + 1], (8, LANES))
+        feat_ref[at, :] = raw_ref[at, :] * scale
+
+
 def kernel(
     ny, nz, gen_early, gen_first,
     train_ref, val_ref, m1_ref, m2_ref, rows_ref, cols_ref, off_ref,
-    feat_ref, scores_ref,
-    row_b, train_in, val_out, val_in, g_ref, tiles,
+    raw_ref, message_ref,
+    row_b, train_in, val_out, val_in, g_ref, tiles, late_tiles,
     core_out, core_in, own, r_out, r_in, x_out, x_in, x_sum, y_out, y_in, y_own, z_out, z_in, yz_out, yz_in,
     g1_out, g1_in, g2_out, g2_in,
     in_send, in_recv, in_local, core_send, core_recv, r_send, r_recv, x_send, x_recv, y_send, y_recv, z_send, z_recv, yz_send, yz_recv,
@@ -104,9 +131,9 @@
     def distance(k):
         return jnp.where(k == 0, 2, jnp.where(k == 1, 1, jnp.where(k == 2, 3, 0)))
 
-    def generate(t):
+    def generate(t, dest, at):
         cols = tile_features(t // NX, distance(lax.rem(t, NX)))
-        make_entries(row_b, cols, offset, tiles.at[t // 2], depth, lax.rem(t, 2) * (2 * LANES))
+        make_entries(row_b, cols, offset, dest.at[at // 2], depth, lax.rem(at, 2) * (2 * LANES))
 
     half = depth // 2
     for d in range(ny):
@@ -119,9 +146,9 @@
         else:
             val_out[d - 1] = stacked
 
-    lax.fori_loop(0, gen_early, lambda t, c: (generate(t), c)[1], 0)
+    lax.fori_loop(0, gen_early, lambda t, c: (generate(t, tiles, t), c)[1], 0)
     pl.semaphore_wait(barrier, len(peers))
-    for d in range(1, ny):
+    for d in sorted(range(1, ny), key=lambda d: -min(d, ny - d)):
         train_copy(d, y0).start()
         val_copy(d, y0).start()
     local_copy = pltpu.make_async_copy(
@@ -129,7 +156,7 @@
     )
     local_copy.start()
 
-    lax.fori_loop(gen_early, gen_first, lambda t, c: (generate(t), c)[1], 0)
+    lax.fori_loop(gen_early, gen_first, lambda t, c: (generate(t, tiles, t), c)[1], 0)
 
     local_copy.wait()
     for d in range(1, ny):
@@ -187,10 +214,10 @@
         peer = (lax.rem(y0 + dy, ny), par_of(lax.rem(z0 + nz - 1, nz), x0, c0))
         return remote(yz_out.at[dy], yz_in.at[dy], yz_send.at[dy], yz_recv.at[dy], peer)
 
-    def multiply(i):
+    def multiply(i, source):
         lhs = jnp.concatenate([g_ref[b] for b in range(groups)], axis=1)
         for pair in range(2):
-            part = jnp.dot(lhs, tiles[i * 2 + pair], preferred_element_type=jnp.float32)
+            part = jnp.dot(lhs, source(pair), preferred_element_type=jnp.float32)
             for k in range(2):
                 at = 2 * k * LANES
                 own[i, pair * 2 + k] = part[:, at : at + LANES]
@@ -263,19 +290,21 @@
 
     def passed_on(i):
         stage(i, CORE_LAG, after_core, nz)
+        stage(i, RELAY_LAG, after_relay, nz)
         stage(i, Y_LAG, after_y, nz - 2)
         stage(i, X_LAG, after_x, nz)
-        stage(i, RELAY_LAG, after_relay, nz)
+
+    mix_from = 0
 
     def with_gen(i, carry):
         for k in range(2):
-            generate(gen_first + i * 2 + k)
-        multiply(i)
+            generate(gen_first + (i - mix_from) * 2 + k, late_tiles, (i - mix_from) * 2 + k)
+        multiply(i, lambda pair: tiles[i * 2 + pair])
         passed_on(i)
         return carry
 
     def without_gen(i, carry):
-        multiply(i)
+        multiply(i, lambda pair: tiles[i * 2 + pair])
         passed_on(i)
         return carry
 
@@ -284,8 +313,11 @@
         return carry
 
     gen_steps = (nz * NX - gen_first) // 2
-    lax.fori_loop(0, gen_steps, with_gen, 0)
-    lax.fori_loop(gen_steps, nz, without_gen, 0)
+    lax.fori_loop(mix_from, mix_from + gen_steps, with_gen, 0)
+    lax.fori_loop(mix_from + gen_steps, nz - 2, without_gen, 0)
+    for i in (nz - 2, nz - 1):
+        multiply(i, lambda pair: late_tiles[(i - nz + 2) * 2 + pair])
+        passed_on(jnp.int32(i))
     lax.fori_loop(nz, nz - 2 + Y_LAG, rest, 0)
     total = y_total(nz - 1)
     for i in range(nz - 2):
@@ -352,32 +384,16 @@
         for dy in range(ny):
             yz_copy(dy).wait_send()
 
-    def turned(a, by):
-        return jnp.concatenate([a[:, LANES - by :], a[:, : LANES - by]], axis=1)
-
     part = all_val // 2
-    lower = lax.rem(lax.broadcasted_iota(jnp.int32, (8, LANES), 1), all_val) < part
-    odd = lax.rem(block, 2) == 1
+    lower, odd = lane_masks(all_val)
     squares = jnp.where(lower, packed(train_sq), jnp.where(odd, val_sq, turned(val_sq, part)))
     message = jnp.concatenate([packed(inner), squares], axis=0)
     near = [(y0, par_of(z0, lax.rem(x0 + d, NX), c)) for d in range(NX) for c in (c0, 1 - c0)][1:]
     message, copies1 = share(message, g1_out, g1_in, g1_send, g1_recv, near, all_sent)
     far = [(y0, par_of(lax.rem(z0 + d, nz), x0, c0)) for d in range(1, nz)]
     message, copies2 = share(message, g2_out, g2_in, g2_send, g2_recv, far, lambda: None)
-    inverse = lax.rsqrt(message[8:] / K + 1e-06)
-    before = turned(inverse, part)
-    train_inv = jnp.where(lower, inverse, before)
-    val_inv = jnp.where(
-        odd, jnp.where(lower, before, inverse),
-        jnp.where(lower, turned(inverse, LANES - part), turned(inverse, LANES - 2 * part)),
-    )
-    scores = message[:8] * train_inv * val_inv * (1.0 / K)
-    for b in range(TRAIN_ROWS // 8):
-        at = slice(b * 8, (b + 1) * 8)
-        scores_ref[at, :] = scores[:, b * all_val : (b + 1) * all_val]
-        scale = jnp.broadcast_to(train_inv[:, b * all_val : b * all_val + 1], (8, LANES))
-        feat_ref[at, :] = trains[at] * scale
-
+    raw_ref[...] = trains
+    message_ref[...] = message
     for copy in copies1 + copies2:
         copy.wait_send()
 
@@ -389,15 +405,15 @@
     all_rows = ny * (TRAIN_ROWS + VAL_ROWS)
     piece = TRAIN_ROWS + ny * VAL_ROWS
     tiles = nz * NX
-    gen_early, gen_first = tiles // 4, 2 * (tiles * 13 // 32)
+    gen_early, gen_first = 6, tiles - 8
     vmem = pl.BlockSpec(memory_space=pltpu.VMEM)
     f32, bf16 = jnp.float32, jnp.bfloat16
     dma = pltpu.SemaphoreType.DMA
-    return pl.pallas_call(
+    raw, message = pl.pallas_call(
         functools.partial(kernel, ny, nz, gen_early, gen_first),
         out_shape=(
             jax.ShapeDtypeStruct((TRAIN_ROWS, LANES), f32),
-            jax.ShapeDtypeStruct((TRAIN_ROWS, ny * VAL_ROWS), f32),
+            jax.ShapeDtypeStruct((16, LANES), f32),
         ),
         in_specs=[pl.BlockSpec(memory_space=pl.ANY)] + [vmem] * 5 + [pl.BlockSpec(memory_space=pltpu.SMEM)],
         out_specs=(vmem, vmem),
@@ -407,7 +423,8 @@
             pltpu.VMEM((ny - 1, 2 * VAL_ROWS, depth // 2), bf16),
             pltpu.VMEM((ny, 2 * VAL_ROWS, depth // 2), bf16),
             pltpu.VMEM((depth // LANES, all_rows, LANES), bf16),
-            pltpu.VMEM((tiles // 2, depth, 4 * LANES), bf16),
+            pltpu.VMEM((tiles // 2 - 4, depth, 4 * LANES), bf16),
+            pltpu.VMEM((4, depth, 4 * LANES), bf16),
             pltpu.VMEM((nz, NX, all_rows, LANES), f32),
             pltpu.VMEM((nz, NX, all_rows, LANES), f32),
             pltpu.VMEM((nz, NX, all_rows, LANES), f32),
@@ -445,6 +462,16 @@
         train, val, m1.reshape(1, local), m2.reshape(1, local),
         rows.reshape(local // LANES, LANES), cols.reshape(1, cols.shape[0]), off,
     )
+    return pl.pallas_call(
+        functools.partial(finish, ny * VAL_ROWS),
+        out_shape=(
+            jax.ShapeDtypeStruct((TRAIN_ROWS, LANES), f32),
+            jax.ShapeDtypeStruct((TRAIN_ROWS, ny * VAL_ROWS), f32),
+        ),
+        in_specs=[vmem, vmem],
+        out_specs=(vmem, vmem),
+        name="finish",
+    )(raw, message)
 
 
 def solution(mesh):

time: 63 us -> 62 us (0.984)
  local copies, waits for them, and re-layouts: 1.94 us -> 0 us
  Pallas kernels: 59.6 us -> 60.5 us
    unnamed x4 -> x0, local copies, waits for them, and re-layouts: 1.94 us -> none
    pallas_call x0 -> x1, Pallas kernels: none -> 1.48 us  [per_device(): pl.pallas_call(functools.partial(finish, ny * VAL_ROWS), out_shape=(jax.S...]
where the time goes in v3:
time: 62 us; the launch traced here: 61.8 us
  Pallas kernels  60.5 us (98%)
  between operations  1.29 us (2%)
    pallas_call x1, Pallas kernels, per_device(): pl.pallas_call(functools.partial(kernel, ny, nz, gen_early, gen_first), o...  59 us
    pallas_call x1, Pallas kernels, per_device(): pl.pallas_call(functools.partial(finish, ny * VAL_ROWS), out_shape=(jax.S...  1.48 us

profile of v3, /device:TPU:1, one launch (start us, length us, event | category | flops | bytes accessed | tf_op | source)
XLA Modules:
  0.0 61.8 jit_solution(687621799066503183)
XLA Ops:
  1.3 59.0 %project.1 = (f32[32,128]{1,0:T(8,128)}, f32[16,128]{1,0:T(8,128)}) custom-call(bf16[32,8192]{1,0:T(8,128)(2,1)} %train_ref.1, bf16[8,8192]{1,0:T(8,128)(2,1)} %val_ref.1, f32[1,8192]{1,0:T(1,128)} %bitcast.4, f32[1,8192]{1,0:T(1,128)} %bitcast.5, s32[64,128]{1,0:T(8,128)} %bitcast.6, s32[1,8192]{1,0:T(1,128)} %bitcast.7, s32[1]{0:T(128)S(6)} %copy.9.off_ref), custom_call_target="tpu_custom_call" | custom-call | tf_op jit(solution)/shard_map/project/pallas_call | solution.py:412
  60.3 1.5 %finish.1 = (f32[32,128]{1,0:T(8,128)}, f32[32,32]{1,0:T(8,128)}) custom-call(f32[32,128]{1,0:T(8,128)} %get-tuple-element.4.raw_ref, f32[16,128]{1,0:T(8,128)} %get-tuple-element.5.message_ref), custom_call_target="tpu_custom_call" | custom-call | tf_op jit(solution)/shard_map/finish/pallas_call | solution.py:465

commit v4 on v3

--- a/solution.py
+++ b/solution.py
@@ -333,10 +333,11 @@
     wide = jnp.concatenate([vals] * fold, axis=0)
     dims = (((1,), (1,)), ((), ()))
     inner = lax.dot_general(trains, wide, dims, precision=lax.Precision.HIGHEST, preferred_element_type=jnp.float32)
-    val_sq = lax.dot_general(
-        jnp.ones((8, LANES), jnp.float32), wide * wide, dims,
-        precision=lax.Precision.HIGHEST, preferred_element_type=jnp.float32,
-    )
+    by_row = jnp.broadcast_to(jnp.sum(vals * vals, axis=1, keepdims=True), (all_val, LANES))
+    row = lax.broadcasted_iota(jnp.int32, (all_val, LANES), 0)
+    lane = lax.broadcasted_iota(jnp.int32, (all_val, LANES), 1)
+    val_sq = jnp.sum(jnp.where(lax.rem(lane, all_val) == row, by_row, 0.0), axis=0, keepdims=True)
+    val_sq = jnp.broadcast_to(val_sq, (8, LANES))
     train_sq = jnp.broadcast_to(jnp.sum(trains * trains, axis=1, keepdims=True), (TRAIN_ROWS, LANES))
     block = lax.broadcasted_iota(jnp.int32, (8, LANES), 1) // all_val
 

time: 62 us -> 61.8 us (level)
  no operation moved by 1% of the time
where the time goes in v4:
time: 61.8 us; the launch traced here: 61.6 us
  Pallas kernels  60.3 us (98%)
  between operations  1.29 us (2%)
    pallas_call x1, Pallas kernels, per_device(): pl.pallas_call(functools.partial(kernel, ny, nz, gen_early, gen_first), o...  58.9 us
    pallas_call x1, Pallas kernels, per_device(): pl.pallas_call(functools.partial(finish, ny * VAL_ROWS), out_shape=(jax.S...  1.48 us

profile of v4, /device:TPU:1, one launch (start us, length us, event | category | flops | bytes accessed | tf_op | source)
XLA Modules:
  0.0 61.6 jit_solution(5082094105699703868)
XLA Ops:
  1.3 58.9 %project.1 = (f32[32,128]{1,0:T(8,128)}, f32[16,128]{1,0:T(8,128)}) custom-call(bf16[32,8192]{1,0:T(8,128)(2,1)} %train_ref.1, bf16[8,8192]{1,0:T(8,128)(2,1)} %val_ref.1, f32[1,8192]{1,0:T(1,128)} %bitcast.4, f32[1,8192]{1,0:T(1,128)} %bitcast.5, s32[64,128]{1,0:T(8,128)} %bitcast.6, s32[1,8192]{1,0:T(1,128)} %bitcast.7, s32[1]{0:T(128)S(6)} %copy.9.off_ref), custom_call_target="tpu_custom_call" | custom-call | tf_op jit(solution)/shard_map/project/pallas_call | solution.py:413
  60.1 1.5 %finish.1 = (f32[32,128]{1,0:T(8,128)}, f32[32,32]{1,0:T(8,128)}) custom-call(f32[32,128]{1,0:T(8,128)} %get-tuple-element.4.raw_ref, f32[16,128]{1,0:T(8,128)} %get-tuple-element.5.message_ref), custom_call_target="tpu_custom_call" | custom-call | tf_op jit(solution)/shard_map/finish/pallas_call | solution.py:466

commit v5 on v4

--- a/solution.py
+++ b/solution.py
@@ -406,7 +406,7 @@
     all_rows = ny * (TRAIN_ROWS + VAL_ROWS)
     piece = TRAIN_ROWS + ny * VAL_ROWS
     tiles = nz * NX
-    gen_early, gen_first = 6, tiles - 8
+    gen_early, gen_first = 7, tiles - 8
     vmem = pl.BlockSpec(memory_space=pltpu.VMEM)
     f32, bf16 = jnp.float32, jnp.bfloat16
     dma = pltpu.SemaphoreType.DMA

time: 61.8 us -> 62.1 us (level)
  no operation moved by 1% of the time
where the time goes in v5:
time: 62.1 us; the launch traced here: 61.9 us
  Pallas kernels  60.6 us (98%)
  between operations  1.29 us (2%)
    pallas_call x1, Pallas kernels, per_device(): pl.pallas_call(functools.partial(kernel, ny, nz, gen_early, gen_first), o...  59.1 us
    pallas_call x1, Pallas kernels, per_device(): pl.pallas_call(functools.partial(finish, ny * VAL_ROWS), out_shape=(jax.S...  1.48 us

profile of v5, /device:TPU:1, one launch (start us, length us, event | category | flops | bytes accessed | tf_op | source)
XLA Modules:
  0.0 61.9 jit_solution(12003430301743760746)
XLA Ops:
  1.3 59.1 %project.1 = (f32[32,128]{1,0:T(8,128)}, f32[16,128]{1,0:T(8,128)}) custom-call(bf16[32,8192]{1,0:T(8,128)(2,1)} %train_ref.1, bf16[8,8192]{1,0:T(8,128)(2,1)} %val_ref.1, f32[1,8192]{1,0:T(1,128)} %bitcast.4, f32[1,8192]{1,0:T(1,128)} %bitcast.5, s32[64,128]{1,0:T(8,128)} %bitcast.6, s32[1,8192]{1,0:T(1,128)} %bitcast.7, s32[1]{0:T(128)S(6)} %copy.9.off_ref), custom_call_target="tpu_custom_call" | custom-call | tf_op jit(solution)/shard_map/project/pallas_call | solution.py:413
  60.4 1.5 %finish.1 = (f32[32,128]{1,0:T(8,128)}, f32[32,32]{1,0:T(8,128)}) custom-call(f32[32,128]{1,0:T(8,128)} %get-tuple-element.4.raw_ref, f32[16,128]{1,0:T(8,128)} %get-tuple-element.5.message_ref), custom_call_target="tpu_custom_call" | custom-call | tf_op jit(solution)/shard_map/finish/pallas_call | solution.py:466
